TPU v7x, 128 devices: a whole 4x4x4 slice. The times are simulated.
128 devices in a mesh: facet: 4 (over y), pix: 8 (over z, core), chan: 4 (over x).
Axes of the slice: x: 4, y: 4, z: 4, core: 2. Of those that a mesh axis runs over, the one named last changes fastest.
Arguments:
- facets: float32 [4, 24, 1024, 1024], P('facet', 'pix', None, 'chan'), may hold values from -600 to 600, as said below
- profiles: float32 [8, 1024], replicated, may hold values from 0.25 to 1
- profile_index: int32 [4, 24], P('facet', 'pix'), may hold values from 0 to 7
Outputs:
- summed_facets: float32 [4, 24, 1024, 1024], P('facet', 'pix', None, 'chan')
Inputs may be any that keep to these rules, and one draw needn't show every extreme that they name: `facets`: real-valued image cubes whose pixels and channels have different scales.
All inputs are finite; a program needn't handle non-finite values.
Results may differ from a plain program's by a relative error of at most 0.0001.
Values sent between devices are 32-bit elements; how exact they have to be, the bound alone decides.
A program may use at most 64 MiB of HBM per device.

v0:
```python
import jax
import jax.numpy as jnp
from jax import lax
from jax.sharding import PartitionSpec as P

OV = 128
ITERS = 4


highest = lax.Precision.HIGHEST
epsilon = 1e-06


def extended(block, sides, width):
    for axis, dim in sides:
        count = lax.axis_size(axis)
        forward = [(i, i + 1) for i in range(count - 1)]
        backward = [(target, source) for source, target in forward]
        low = lax.ppermute(
            lax.slice_in_dim(block, block.shape[dim] - width, None, axis=dim), axis, forward
        )
        high = lax.ppermute(lax.slice_in_dim(block, 0, width, axis=dim), axis, backward)
        block = jnp.concatenate([low, block, high], axis=dim)
    return block


def gather_iterate(current):
    return lax.all_gather(current, ("pix", "chan"), axis=0, tiled=True)


def identity_rows(count, channels, row_start):
    column_ids = lax.broadcasted_iota(jnp.int32, (count, channels), 1)
    row_ids = lax.broadcasted_iota(jnp.int32, (count, channels), 0) + row_start
    return (column_ids == row_ids).astype(jnp.float32)


def body(facets, profiles, profile_index):
    local_cube = facets[0]
    rows_dev, columns, chans_dev = local_cube.shape
    profile_count = profiles.shape[0]
    onehot = (
        profile_index[0][:, None] == jnp.arange(profile_count, dtype=jnp.int32)[None, :]
    ).astype(jnp.float32)
    weight = jnp.dot(onehot, profiles, precision=highest, preferred_element_type=jnp.float32)
    weighted = (local_cube * weight[:, :, None]).reshape(rows_dev * columns, chans_dev)
    spectra = lax.all_to_all(weighted, "chan", split_axis=0, concat_axis=1, tiled=True)
    channels = spectra.shape[1]
    per_device = channels // (lax.axis_size("pix") * lax.axis_size("chan"))
    row_start = lax.axis_index(("pix", "chan")) * per_device
    gram_block = lax.psum_scatter(
        lax.dot_general(
            spectra,
            spectra,
            (((0,), (0,)), ((), ())),
            precision=highest,
            preferred_element_type=jnp.float32,
        ),
        ("pix", "chan"),
        scatter_dimension=0,
        tiled=True,
    )
    block_identity = identity_rows(per_device, channels, row_start)
    own_identity = identity_rows(gram_block.shape[0], channels, row_start)
    trace_part = jnp.sum(gram_block * own_identity)
    square_part = jnp.sum(gram_block * gram_block)
    trace_total, square_total = lax.psum((trace_part, square_part), ("pix", "chan"))
    mean_eig = trace_total / channels
    spread = jnp.sqrt(square_total - trace_total * trace_total / channels + epsilon)
    current = (gram_block - mean_eig * block_identity) / spread
    identity = jnp.eye(channels, dtype=jnp.float32)
    gathered = current
    for iteration in range(ITERS + 1):
        gathered = gather_iterate(current)
        if iteration < ITERS:
            square = jnp.dot(
                current, gathered, precision=highest, preferred_element_type=jnp.float32
            )
            cubic = jnp.dot(square, gathered, precision=highest, preferred_element_type=jnp.float32)
            current = 1.5 * current - 0.5 * cubic
    project = 0.5 * (identity + gathered)
    result = jnp.dot(spectra, project, precision=highest, preferred_element_type=jnp.float32)
    returned = lax.all_to_all(result, "chan", split_axis=1, concat_axis=0, tiled=True)
    picture = returned.reshape(rows_dev, columns, chans_dev) * weight[:, :, None]
    padded = extended(picture, (("facet", 1),), OV)
    from_left = padded[:, :OV]
    from_right = padded[:, columns + OV :]
    total = picture.at[:, :OV].add(from_left)
    total = total.at[:, columns - OV :].add(from_right)
    return total[None]


def solution(mesh):
    return jax.shard_map(
        body,
        mesh=mesh,
        in_specs=(P("facet", "pix", None, "chan"), P(), P("facet", "pix")),
        out_specs=P("facet", "pix", None, "chan"),
        check_vma=False,
    )
```

profile of v0, /device:TPU:1, one launch (start us, length us, event | category | flops | bytes accessed | tf_op | source)
XLA Modules:
  0.0 569.5 jit_solution(7450465616782517902)
XLA Ops:
  6.5 0.0 copy-start
  6.5 0.0 reduce-scatter.2.cloned.1.call-start
  6.5 0.8 copy-done
  7.3 0.9 fusion.6
  8.2 2.4 broadcast_multiply_fusion.1
  10.5 41.3 %all_to_all.29 = f32[4,768,256]{2,1,0:T(8,128)S(1)} all-to-all(f32[4,768,256]{2,1,0:T(8,128)S(1)} %broadcast_multiply_fusion.1), channel_id=1, replica_groups=mesh['facet'=4,'pix'=8,'chan'=4] {'chan'}, dimensions={0} | all-to-all | bytes 6291456 | tf_op jit(solution)/shard_map/all_to_all | solution.py:46
  51.8 0.4 copy.10
  52.2 11.7 %fusion.9 = f32[1024,1024]{1,0:T(8,128)} fusion(f32[768,1024]{1,0:T(8,128)S(1)} %bitcast.42), kind=kOutput, calls=%fused_computation.25 | convolution fusion | flops 9663676416 | bytes 7340032 | tf_op jit(solution)/shard_map/dot_general | solution.py:51
  63.9 0.0 reduce-scatter.2.cloned.1.call-update
  63.9 0.0 all-gather.6.cloned.1.call-start
  64.0 82.2 %reduce-scatter.2.cloned.1.call-done = f32[32,1024]{1,0:T(8,128)} async-done(((f32[1024,1024]{1,0:T(8,128)}), f32[32,1024]{1,0:T(8,128)}) %reduce-scatter.2.cloned.1.call-update) | async-done | bytes 131088 | tf_op jit(solution)/shard_map/reduce_scatter | solution.py:50
  146.2 1.6 select_reduce_fusion
  147.8 61.8 %all-reduce = (f32[]{:T(128)}, f32[]{:T(128)}) all-reduce(f32[]{:T(128)} %get-tuple-element.30, f32[]{:T(128)} %get-tuple-element.29), channel_id=1, replica_groups=mesh['facet'=4,'pix'=8,'chan'=4] {'pix','chan'}, use_global_device_ids=true, to_apply=%region_4.0 | all-reduce | flops 2 | bytes 16 | tf_op jit(solution)/shard_map/psum | solution.py:66
  212.3 1.6 subtract_divide_fusion
  213.9 0.0 copy-start.9
  213.9 0.0 all-gather.6.cloned.1.call-update
  214.0 0.0 all-gather.8.cloned.1.call-start
  214.0 48.0 %all-gather.6.cloned.1.call-done = f32[1024,1024]{1,0:T(8,128)} async-done(((f32[32,1024]{1,0:T(8,128)}), f32[1024,1024]{1,0:T(8,128)}) %all-gather.6.cloned.1.call-update) | async-done | bytes 4194320 | tf_op jit(solution)/shard_map/all_gather | solution.py:28
  262.0 0.0 copy-start.2
  262.0 4.9 fusion.10
  266.9 0.0 copy-done.9
  266.9 0.0 copy-done.2
  266.9 3.1 fusion.3
  270.1 0.0 copy-start.6
  270.1 0.0 all-gather.8.cloned.1.call-update
  270.1 0.2 all-gather.10.cloned.1.call-start
  270.3 45.6 %all-gather.8.cloned.1.call-done = f32[1024,1024]{1,0:T(8,128)} async-done(((f32[32,1024]{1,0:T(8,128)}), f32[1024,1024]{1,0:T(8,128)}) %all-gather.8.cloned.1.call-update) | async-done | bytes 4194320 | tf_op jit(solution)/shard_map/all_gather | solution.py:28
  315.9 0.0 copy-start.3
  315.9 4.9 fusion.11
  320.8 0.0 copy-done.6
  320.8 0.0 copy-done.3
  320.8 3.1 fusion.2
  324.0 0.0 all-gather.10.cloned.1.call-update
  324.0 0.0 all-gather.12.cloned.1.call-start
  324.1 45.8 %all-gather.10.cloned.1.call-done = f32[1024,1024]{1,0:T(8,128)} async-done(((f32[32,1024]{1,0:T(8,128)}), f32[1024,1024]{1,0:T(8,128)}) %all-gather.10.cloned.1.call-update) | async-done | bytes 4194320 | tf_op jit(solution)/shard_map/all_gather | solution.py:28
  369.8 4.9 fusion.12
  374.7 0.0 copy-done.7
  374.7 0.0 copy-done.4
  374.8 3.1 fusion.1
  377.9 0.0 all-gather.12.cloned.1.call-update
  377.9 0.3 all-gather.14.cloned.1.call-start
  378.2 45.5 %all-gather.12.cloned.1.call-done = f32[1024,1024]{1,0:T(8,128)} async-done(((f32[32,1024]{1,0:T(8,128)}), f32[1024,1024]{1,0:T(8,128)}) %all-gather.12.cloned.1.call-update) | async-done | bytes 4194320 | tf_op jit(solution)/shard_map/all_gather | solution.py:28
  423.7 4.9 fusion.13
  428.6 0.0 copy-done.8
  428.6 0.0 copy-done.5
  428.7 3.1 fusion
  431.8 0.0 all-gather.14.cloned.1.call-update
  431.8 3.7 copy.7
  435.5 3.5 reshape.86
  439.1 38.6 %all-gather.14.cloned.1.call-done = f32[1024,1024]{1,0:T(8,128)} async-done(((f32[32,1024]{1,0:T(8,128)}), f32[1024,1024]{1,0:T(8,128)}) %all-gather.14.cloned.1.call-update) | async-done | bytes 4194320 | tf_op jit(solution)/shard_map/all_gather | solution.py:28
  477.6 5.0 multiply_bitcast_fusion
  482.7 5.3 copy.9
  488.0 11.9 %fusion.14 = f32[768,4,256]{2,0,1:T(8,128)S(1)} fusion(f32[768,1024,1]{1,0,2:T(8,128)S(1)} %reshape.86, f32[4,256,1024]{2,1,0:T(8,128)} %bitcast.41), kind=kOutput, calls=%fused_computation.30 | convolution fusion | flops 9663676416 | bytes 10485760 | tf_op jit(solution)/shard_map/dot_general | solution.py:81
  499.9 40.0 %all_to_all.30 = f32[768,4,256]{2,0,1:T(8,128)S(1)} all-to-all(f32[768,4,256]{2,0,1:T(8,128)S(1)} %fusion.14), channel_id=1, replica_groups=mesh['facet'=4,'pix'=8,'chan'=4] {'chan'}, dimensions={1} | all-to-all | bytes 6291456 | tf_op jit(solution)/shard_map/all_to_all | solution.py:82
  540.0 0.5 broadcast_multiply_fusion
  540.4 0.0 copy-start.1
  540.5 3.1 collective-permute-start
  543.6 7.0 %collective-permute-done = f32[3,128,256]{2,1,0:T(8,128)S(1)} collective-permute-done((f32[3,128,256]{2,1,0:T(8,128)S(1)}, f32[3,128,256]{2,1,0:T(8,128)S(1)}, u32[]{:S(2)}, u32[]{:S(2)}) %collective-permute-start) | collective-permute-done | bytes 393248 | tf_op jit(solution)/shard_map/ppermute | solution.py:19
  550.6 0.1 fusion.8
  550.7 1.3 collective-permute-start.1
  552.0 1.7 copy.12
  553.6 8.2 %collective-permute-done.1 = f32[3,128,256]{2,1,0:T(8,128)S(1)} collective-permute-done((f32[3,128,256]{2,1,0:T(8,128)S(1)}, f32[3,128,256]{2,1,0:T(8,128)S(1)}, u32[]{:S(2)}, u32[]{:S(2)}) %collective-permute-start.1) | collective-permute-done | bytes 393248 | tf_op jit(solution)/shard_map/ppermute | solution.py:22
  561.9 0.8 fusion.5
  562.7 0.0 copy-done.1
  (7 shorter events, 0.1 us)
Async XLA Ops:
  6.5 0.8 copy-start
  6.5 139.7 %reduce-scatter.2.cloned.1.call-start = ((), (), s32[]{:S(2)}) async-start(), calls=%async_computation.3 | async-start | bytes 4325376 | tf_op jit(solution)/shard_map/reduce_scatter | solution.py:50
  63.9 198.1 %all-gather.6.cloned.1.call-start = ((), (), s32[]{:S(2)}) async-start(), calls=%async_computation.4 | async-start | bytes 4325376 | tf_op jit(solution)/shard_map/all_gather | solution.py:28
  213.9 53.0 %copy-start.9 = (f32[32,1024]{1,0:T(8,128)S(1)}, f32[32,1024]{1,0:T(8,128)}, u32[]{:S(2)}) copy-start(f32[32,1024]{1,0:T(8,128)} %subtract_divide_fusion) | copy-start | bytes 393220
  214.0 102.0 %all-gather.8.cloned.1.call-start = ((), (), s32[]{:S(2)}) async-start(), calls=%async_computation.5 | async-start | bytes 4325376 | tf_op jit(solution)/shard_map/all_gather | solution.py:28
  262.0 4.9 copy-start.2
  270.1 50.7 %copy-start.6 = (f32[32,1024]{1,0:T(8,128)S(1)}, f32[32,1024]{1,0:T(8,128)}, u32[]{:S(2)}) copy-start(f32[32,1024]{1,0:T(8,128)} %fusion.3) | copy-start | bytes 393220
  270.1 99.7 %all-gather.10.cloned.1.call-start = ((), (), s32[]{:S(2)}) async-start(), calls=%async_computation.6 | async-start | bytes 4325376 | tf_op jit(solution)/shard_map/all_gather | solution.py:28
  315.9 4.9 copy-start.3
  324.0 50.7 %copy-start.7 = (f32[32,1024]{1,0:T(8,128)S(1)}, f32[32,1024]{1,0:T(8,128)}, u32[]{:S(2)}) copy-start(f32[32,1024]{1,0:T(8,128)} %fusion.2) | copy-start | bytes 393220
  324.0 99.7 %all-gather.12.cloned.1.call-start = ((), (), s32[]{:S(2)}) async-start(), calls=%async_computation.7 | async-start | bytes 4325376 | tf_op jit(solution)/shard_map/all_gather | solution.py:28
  369.8 4.9 copy-start.4
  377.9 50.7 %copy-start.8 = (f32[32,1024]{1,0:T(8,128)S(1)}, f32[32,1024]{1,0:T(8,128)}, u32[]{:S(2)}) copy-start(f32[32,1024]{1,0:T(8,128)} %fusion.1) | copy-start | bytes 393220
  377.9 99.7 %all-gather.14.cloned.1.call-start = ((), (), s32[]{:S(2)}) async-start(), calls=%async_computation.8 | async-start | bytes 4325376 | tf_op jit(solution)/shard_map/all_gather | solution.py:28
  423.7 4.9 copy-start.5
  540.4 22.2 %copy-start.1 = (f32[8,1024]{1,0:T(8,128)S(1)}, f32[8,1024]{1,0:T(8,128)}, u32[]{:S(2)}) copy-start(f32[8,1024]{1,0:T(8,128)} %param.8) | copy-start | bytes 98308
  540.5 10.1 %collective-permute-start = (f32[3,128,256]{2,1,0:T(8,128)S(1)}, f32[3,128,256]{2,1,0:T(8,128)S(1)}, u32[]{:S(2)}, u32[]{:S(2)}) collective-permute-start(f32[3,128,256]{2,1,0:T(8,128)S(1)} %slice.56), channel_id=1, source_target_pairs={{0,32},{32,64},{64,96},{1,33},{33,65},{65,97},{2,34},{34,66},{66,9... | collective-permute-start | bytes 1179656 | tf_op jit(solution)/shard_map/ppermute | solution.py:19
  550.7 11.2 %collective-permute-start.1 = (f32[3,128,256]{2,1,0:T(8,128)S(1)}, f32[3,128,256]{2,1,0:T(8,128)S(1)}, u32[]{:S(2)}, u32[]{:S(2)}) collective-permute-start(f32[3,128,256]{2,1,0:T(8,128)S(1)} %get-tuple-element.33), channel_id=1, source_target_pairs={{32,0},{64,32},{96,64},{33,1},{65,33},{97,65},{34,2},{66,34},{98,6... | collective-permute-start | bytes 1179656 | tf_op jit(solution)/shard_map/ppermute | solution.py:22
Sparse Core Ops, SparseCore 0:
  64.0 82.1 reduce-scatter.1
  214.1 47.9 all-gather.5
  270.2 45.6 all-gather.7
  324.1 45.6 all-gather.9
  378.0 45.6 all-gather.11
  431.9 45.6 all-gather.13
where the time goes:
time: 572 us; the launch traced here: 570 us
  waiting for transfers between devices  321 us (56%)
  blocking collectives  143 us (25%)
  matrix products  56.5 us (10%)
  between operations  16.3 us (3%)
  local copies, waits for them, and re-layouts  15.5 us (3%)
  other arithmetic  12.1 us (2%)
    all_gather x5, waiting for transfers between devices, gather_iterate(): return lax.all_gather(current, ('pix', 'chan'), axis=0, tiled=True)  224 us
    reduce_scatter x1, waiting for transfers between devices, body(): lax.psum_scatter(lax.dot_general(spectra, spectra, (((0,), (0,)), ((), ()...  82.2 us
    psum x1, blocking collectives, body(): lax.psum((trace_part, square_part), ('pix', 'chan'))  61.8 us
    all_to_all x1, blocking collectives, body(): lax.all_to_all(weighted, 'chan', split_axis=0, concat_axis=1, tiled=True)  41.3 us
    all_to_all x1, blocking collectives, body(): lax.all_to_all(result, 'chan', split_axis=1, concat_axis=0, tiled=True)  40 us
    dot_general x4, matrix products, body(): jnp.dot(current, gathered, precision=highest, preferred_element_type=jnp....  19.5 us
    dot_general x4, matrix products, body(): jnp.dot(square, gathered, precision=highest, preferred_element_type=jnp.f...  12.6 us
    dot_general x1, matrix products, body(): jnp.dot(spectra, project, precision=highest, preferred_element_type=jnp.f...  11.9 us
  transfers between devices with their start and end apart: 8, of which 8 were waited for; matrix products, arithmetic and copies ran while one was open for 2% of the time, Pallas kernels for 0%

commit v1 on v0

v1 whole, which is shorter than its diff:
```python
import functools

import jax
import jax.numpy as jnp
from jax import lax
from jax.experimental import pallas as pl
from jax.experimental.pallas import tpu as pltpu
from jax.sharding import PartitionSpec as P

OV = 128
ITERS = 4
EPSILON = 1e-06
MESH = pl.DeviceIdType.MESH
BF16 = jnp.bfloat16
F32 = jnp.float32

ROWS = 3
COLS = 1024
BLOCK = 256
HALF = 128
BLOCKS = 4
CHANNELS = BLOCK * BLOCKS
PIXELS = ROWS * BLOCK
PAIRS = [(0, 0), (1, 1), (2, 2), (3, 3), (0, 1), (1, 2), (2, 3), (3, 0), (0, 2), (1, 3)]
TILES = len(PAIRS)


def dot(a, b):
    return lax.dot_general(a, b, (((1,), (0,)), ((), ())), preferred_element_type=F32)


def dot3(a_high, a_low, b_high, b_low):
    return dot(a_high, b_high) + dot(a_high, b_low) + dot(a_low, b_high)


def split(value):
    high = value.astype(BF16)
    low = (value - high.astype(F32)).astype(BF16)
    return high, low


def block(i):
    return slice(i * BLOCK, (i + 1) * BLOCK)


def kernel(
    facets, profiles, index, out,
    cube, weight, pix_hl, pix_t_hl, gram, total, from_core, from_z1, from_z2, from_x,
    signs, square, proj, result, border,
    send_near, recv_near, send_far, recv_far, own_sem,
    send_core, recv_core, send_z, recv_z, send_x, recv_x,
    send_xg, recv_xg, send_zg, recv_zg, send_cg, recv_cg,
    send_border, recv_border, out_sem,
):
    f = lax.axis_index("facet")
    p = lax.axis_index("pix")
    a = lax.axis_index("chan")
    z = p // 2
    k = p % 2
    right = (a + 1) % 4
    left = (a + 3) % 4
    across = (a + 2) % 4
    z_up = (z + 1) % 4
    z_down = (z + 3) % 4
    z_across = (z + 2) % 4

    def at_x(chan):
        return (f, p, chan)

    def at_z(zz):
        return (f, zz * 2 + k, a)

    core_mate = (f, z * 2 + (1 - k), a)
    facet_up = ((f + 1) % 4, p, a)
    facet_down = ((f + 3) % 4, p, a)

    barrier = pltpu.get_barrier_semaphore()
    partners = [
        at_x(right), at_x(left), at_x(across), at_z(z_up), at_z(z_down), core_mate, facet_up, facet_down,
    ]
    for partner in partners:
        pl.semaphore_signal(barrier, inc=1, device_id=partner, device_id_type=MESH)
    pl.semaphore_wait(barrier, len(partners))

    def remote(src, dst, send_sem, recv_sem, device):
        return pltpu.make_async_remote_copy(
            src_ref=src, dst_ref=dst, send_sem=send_sem, recv_sem=recv_sem,
            device_id=device, device_id_type=MESH,
        )

    toward = [right, left]
    behind = [left, right]

    def piece(q, h):
        return pl.ds(pl.multiple_of(q * BLOCK + h * HALF, HALF), HALF)

    def near(way, q, h):
        there = cube.at[a, :, piece(q, h), :]
        return remote(
            facets.at[0, :, piece(q, h), :], there,
            send_near.at[way, q, h], recv_near.at[way, q, h], at_x(toward[way]),
        )

    def far(way, q):
        there = cube.at[behind[way], :, piece(q, way), :]
        return remote(there, there, send_far.at[way, q], recv_far.at[way, q], at_x(toward[way]))

    def wait_near(way, q, h):
        there = cube.at[behind[way], :, piece(q, h), :]
        remote(
            there, there, send_near.at[way, q, h], recv_near.at[way, q, h], at_x(toward[way])
        ).wait_recv()

    def wait_far(way, q):
        there = cube.at[across, :, piece(q, way), :]
        remote(there, there, send_far.at[way, q], recv_far.at[way, q], at_x(toward[way])).wait_recv()

    def quarter(way, step):
        if way == 0:
            place = (4 - right) % 4
            n = step + jnp.where(place <= step, 1, 0)
            return (4 - n) % 4
        place = (left + 1) % 4
        n = step + jnp.where(place <= step, 1, 0)
        return (3 + n) % 4

    def near_round(step):
        for way in (0, 1):
            q = quarter(way, step)
            for h in (way, 1 - way):
                if h == way:
                    @pl.when(q != across)
                    def _():
                        near(way, q, h).start()
                else:
                    near(way, q, h).start()

    def far_round(step):
        for way in (0, 1):
            q = quarter(way, step)

            @pl.when(q != a)
            def _():
                wait_near(way, q, way)

            far(way, q).start()

    for way in (0, 1):
        near(way, toward[way], way).start()
    for way in (0, 1):
        near(way, across, way).start()
    for way in (0, 1):
        near(way, toward[way], 1 - way).start()
    own = pltpu.make_async_copy(facets.at[0], cube.at[a], own_sem)
    own.start()

    for r in range(ROWS):
        row = profiles[0:1, :]
        for n in range(1, profiles.shape[0]):
            row = jnp.where(index[0, r] == n, profiles[n : n + 1, :], row)
        weight[r] = jnp.broadcast_to(row, (128, COLS)).T

    own.wait()

    mine = pl.ds(pl.multiple_of(a * BLOCK, BLOCK), BLOCK)

    def spectra(b):
        columns = pl.ds(pl.multiple_of(b * BLOCK, BLOCK), BLOCK)
        for r in range(ROWS):
            w = weight[r, mine, :]
            x = cube[b, r, mine, :] * jnp.concatenate([w, w], axis=1)
            high, low = split(x)
            pix_hl[0, block(r), columns] = high
            pix_hl[1, block(r), columns] = low
            high, low = split(x.T)
            pix_t_hl[0, columns, block(r)] = high
            pix_t_hl[1, columns, block(r)] = low

    spectra(a)
    for way in (0, 1):
        wait_near(way, toward[way], way)
        far(way, toward[way]).start()
    for way in (0, 1):
        wait_near(way, a, 0)
        wait_near(way, a, 1)
    spectra(left)
    spectra(right)
    for way in (0, 1):
        wait_far(way, a)
    near_round(0)
    spectra(across)

    for t, (i, j) in enumerate(PAIRS):
        gram[t] = dot3(
            pix_t_hl[0, block(i), :], pix_t_hl[1, block(i), :], pix_hl[0, :, block(j)], pix_hl[1, :, block(j)]
        )

    def rows(start, count):
        return pl.ds(pl.multiple_of(start, 8), count)

    half = k * 128
    swap = remote(
        gram.at[:, rows((1 - k) * 128, 128), :], from_core, send_core, recv_core, core_mate
    )
    swap.start()
    swap.wait()

    def part(zz):
        return half + zz * 32

    gram[:, rows(half, 128), :] += from_core[...]

    first = [
        remote(gram.at[:, rows(part(z_across), 16), :], from_z1.at[0], send_z.at[0], recv_z.at[0], at_z(z_up)),
        remote(gram.at[:, rows(part(z_across) + 16, 16), :], from_z1.at[1], send_z.at[1], recv_z.at[1], at_z(z_down)),
    ]
    for copy in first:
        copy.start()
    for copy in first:
        copy.wait()
    gram[:, rows(part(z_up), 16), :] += from_z1[0]
    gram[:, rows(part(z_down) + 16, 16), :] += from_z1[1]
    second = [
        remote(gram.at[:, rows(part(z_up), 32), :], from_z2.at[0], send_z.at[2], recv_z.at[2], at_z(z_up)),
        remote(gram.at[:, rows(part(z_down), 32), :], from_z2.at[1], send_z.at[3], recv_z.at[3], at_z(z_down)),
    ]
    for copy in second:
        copy.start()
    for copy in second:
        copy.wait()
    base = part(z)
    gram[:, rows(base, 32), :] += from_z2[0] + from_z2[1]

    scatter = []
    for d in (1, 2, 3):
        target = (a + d) % 4
        scatter.append(remote(
            gram.at[:, rows(base + target * 8, 8), :], from_x.at[d - 1],
            send_x.at[d - 1], recv_x.at[d - 1], at_x(target),
        ))
    for copy in scatter:
        copy.start()
    for copy in scatter:
        copy.wait()
    own_rows = rows(base + a * 8, 8)
    total[:, own_rows, :] = (gram[:, own_rows, :] + from_x[0]) + (from_x[1] + from_x[2])

    def gather_x(d):
        return remote(
            total.at[:, own_rows, :], total.at[:, own_rows, :],
            send_xg.at[d - 1], recv_xg.at[d - 1], at_x((a + d) % 4),
        )

    for d in (1, 2, 3):
        gather_x(d).start()
    for d in (1, 2, 3):
        there = total.at[:, rows(base + ((a + 4 - d) % 4) * 8, 8), :]
        remote(there, there, send_xg.at[d - 1], recv_xg.at[d - 1], at_x((a + d) % 4)).wait_recv()

    def whole(zz):
        return total.at[:, rows(part(zz), 32), :]

    def low_half(zz):
        return total.at[:, rows(part(zz), 16), :]

    def high_half(zz):
        return total.at[:, rows(part(zz) + 16, 16), :]

    def along(ref, slot, device):
        return remote(ref, ref, send_zg.at[slot], recv_zg.at[slot], device)

    def to_mate(ref, slot):
        return remote(ref, ref, send_cg.at[slot], recv_cg.at[slot], core_mate)

    along(whole(z), 0, at_z(z_up)).start()
    along(whole(z), 1, at_z(z_down)).start()
    to_mate(whole(z), 0).start()
    far_round(0)
    near_round(1)
    near_round(2)
    along(whole(z_down), 0, at_z(z_up)).wait_recv()
    along(low_half(z_down), 2, at_z(z_up)).start()
    to_mate(whole(z_down), 1).start()
    along(whole(z_up), 1, at_z(z_down)).wait_recv()
    along(high_half(z_up), 3, at_z(z_down)).start()
    to_mate(whole(z_up), 2).start()
    along(low_half(z_across), 2, at_z(z_up)).wait_recv()
    along(high_half(z_across), 3, at_z(z_down)).wait_recv()
    to_mate(whole(z_across), 3).start()

    def mate_whole(zz):
        return total.at[:, rows((1 - k) * 128 + zz * 32, 32), :]

    for slot, zz in enumerate((z, z_down, z_up, z_across)):
        to_mate(mate_whole(zz), slot).wait_recv()

    eye = (
        lax.broadcasted_iota(jnp.int32, (BLOCK, BLOCK), 0) == lax.broadcasted_iota(jnp.int32, (BLOCK, BLOCK), 1)
    ).astype(F32)

    def add_up(tile):
        return jnp.sum(jnp.sum(tile, axis=0, keepdims=True), axis=1, keepdims=True)

    diagonal = total[0] * eye
    for t in range(1, BLOCKS):
        diagonal = diagonal + total[t] * eye
    mean_eig = add_up(diagonal) / CHANNELS
    squares = None
    for t in range(TILES):
        if t < BLOCKS:
            moved = total[t] - mean_eig * eye
            term = moved * moved
        else:
            term = 2.0 * (total[t] * total[t])
        squares = term if squares is None else squares + term
    spread = jnp.sqrt(add_up(squares) + EPSILON)

    def put(ref, lead, i, j, tile):
        high, low = split(tile)
        ref[lead + (0, block(i), block(j))] = high
        ref[lead + (1, block(i), block(j))] = low
        if i != j:
            high, low = split(tile.T)
            ref[lead + (0, block(j), block(i))] = high
            ref[lead + (1, block(j), block(i))] = low

    for t, (i, j) in enumerate(PAIRS):
        tile = total[t]
        if i == j:
            tile = tile - mean_eig * eye
        tile = tile / spread
        gram[t] = tile
        put(signs, (0,), i, j, tile)

    def iterate(step, _):
        now = step % 2
        later = 1 - now

        @pl.when(step == 1)
        def _():
            far_round(1)

        @pl.when(step == 2)
        def _():
            far_round(2)

        for i, j in PAIRS:
            put(square, (), i, j, dot3(
                signs[now, 0, block(i), :], signs[now, 1, block(i), :],
                signs[now, 0, :, block(j)], signs[now, 1, :, block(j)],
            ))
        for t, (i, j) in enumerate(PAIRS):
            cubic = dot3(
                signs[now, 0, block(i), :], signs[now, 1, block(i), :],
                square[0, :, block(j)], square[1, :, block(j)],
            )
            tile = 1.5 * gram[t] - 0.5 * cubic
            gram[t] = tile
            put(signs, (later,), i, j, tile)
        return 0

    lax.fori_loop(0, ITERS - 1, iterate, 0)

    last = (ITERS - 1) % 2
    for i in range(BLOCKS):
        high, low = split(dot3(
            signs[last, 0, block(i), :], signs[last, 1, block(i), :],
            signs[last, 0, :, mine], signs[last, 1, :, mine],
        ))
        square[0, block(i), 0:BLOCK] = high
        square[1, block(i), 0:BLOCK] = low
    for i in range(BLOCKS):
        cubic = dot3(
            signs[last, 0, block(i), :], signs[last, 1, block(i), :],
            square[0, :, 0:BLOCK], square[1, :, 0:BLOCK],
        )
        current = signs[last, 0, block(i), mine].astype(F32) + signs[last, 1, block(i), mine].astype(F32)
        high, low = split(1.5 * current - 0.5 * cubic)
        proj[0, block(i), :] = high
        proj[1, block(i), :] = low

    def filtered(q):
        @pl.when(q != a)
        def _():
            for way in (0, 1):
                wait_near(way, q, 1 - way)
                wait_far(way, q)

        for r in range(ROWS):
            x = jnp.concatenate([cube[b, r, block(q), :] for b in range(BLOCKS)], axis=1)
            high, low = split(x)
            product = dot3(high, low, proj[0], proj[1])
            w = weight[r, block(q), :]
            w = 0.5 * (w * w)
            result[r, block(q), :] = (cube[a, r, block(q), :] + product) * jnp.concatenate([w, w], axis=1)

    def to_hbm(q):
        there = (slice(None), block(q), slice(None))
        return pltpu.make_async_copy(result.at[there], out.at[(0,) + there], out_sem.at[q])

    low_rim = result.at[:, 0:OV, :]
    high_rim = result.at[:, COLS - OV : COLS, :]
    down = remote(low_rim, border.at[1], send_border.at[0], recv_border.at[0], facet_down)
    up = remote(high_rim, border.at[0], send_border.at[1], recv_border.at[1], facet_up)

    filtered(0)

    @pl.when(f > 0)
    def _():
        down.start()

    filtered(3)

    @pl.when(f < 3)
    def _():
        up.start()

    for q in (1, 2):
        filtered(q)
        to_hbm(q).start()

    @pl.when(f > 0)
    def _():
        down.wait_send()
        up.wait_recv()
        result[:, 0:OV, :] += border[0]

    to_hbm(0).start()

    @pl.when(f < 3)
    def _():
        up.wait_send()
        down.wait_recv()
        result[:, COLS - OV : COLS, :] += border[1]

    to_hbm(3).start()

    for way in (0, 1):
        for q in range(BLOCKS):
            for h in (0, 1):
                near(way, q, h).wait_send()
            far(way, q).wait_send()
    for d in (1, 2, 3):
        gather_x(d).wait_send()
    along(whole(z), 0, at_z(z_up)).wait_send()
    along(whole(z), 1, at_z(z_down)).wait_send()
    along(low_half(z_down), 2, at_z(z_up)).wait_send()
    along(high_half(z_up), 3, at_z(z_down)).wait_send()
    for slot, zz in enumerate((z, z_down, z_up, z_across)):
        to_mate(whole(zz), slot).wait_send()
    for q in range(BLOCKS):
        to_hbm(q).wait()


def body(facets, profiles, profile_index):
    dma = pltpu.SemaphoreType.DMA
    scratch = [
        pltpu.VMEM((BLOCKS, ROWS, COLS, BLOCK), F32),
        pltpu.VMEM((ROWS, COLS, 128), F32),
        pltpu.VMEM((2, PIXELS, CHANNELS), BF16),
        pltpu.VMEM((2, CHANNELS, PIXELS), BF16),
        pltpu.VMEM((TILES, BLOCK, BLOCK), F32),
        pltpu.VMEM((TILES, BLOCK, BLOCK), F32),
        pltpu.VMEM((TILES, 128, BLOCK), F32),
        pltpu.VMEM((2, TILES, 16, BLOCK), F32),
        pltpu.VMEM((2, TILES, 32, BLOCK), F32),
        pltpu.VMEM((3, TILES, 8, BLOCK), F32),
        pltpu.VMEM((2, 2, CHANNELS, CHANNELS), BF16),
        pltpu.VMEM((2, CHANNELS, CHANNELS), BF16),
        pltpu.VMEM((2, CHANNELS, BLOCK), BF16),
        pltpu.VMEM((ROWS, COLS, BLOCK), F32),
        pltpu.VMEM((2, ROWS, OV, BLOCK), F32),
        dma((2, 4, 2)), dma((2, 4, 2)), dma((2, 4)), dma((2, 4)), dma,
        dma, dma, dma((4,)), dma((4,)), dma((3,)), dma((3,)),
        dma((3,)), dma((3,)), dma((4,)), dma((4,)), dma((4,)), dma((4,)),
        dma((2,)), dma((2,)), dma((4,)),
    ]
    return pl.pallas_call(
        kernel,
        out_shape=jax.ShapeDtypeStruct(facets.shape, F32),
        in_specs=[
            pl.BlockSpec(memory_space=pl.ANY),
            pl.BlockSpec(memory_space=pltpu.VMEM),
            pl.BlockSpec(memory_space=pltpu.SMEM),
        ],
        out_specs=pl.BlockSpec(memory_space=pl.ANY),
        scratch_shapes=scratch,
        compiler_params=pltpu.CompilerParams(
            collective_id=0, has_side_effects=True, vmem_limit_bytes=60 * 2**20
        ),
        cost_estimate=pl.CostEstimate(flops=60 * 10**9, bytes_accessed=6 * 2**20, transcendentals=0),
        name="facet_filter",
    )(facets, profiles, profile_index)


def solution(mesh):
    return jax.shard_map(
        body,
        mesh=mesh,
        in_specs=(P("facet", "pix", None, "chan"), P(), P("facet", "pix")),
        out_specs=P("facet", "pix", None, "chan"),
        check_vma=False,
    )
```

time: 572 us -> 147 us (0.26)
  waiting for transfers between devices: 321 us -> 0 us
  blocking collectives: 143 us -> 0 us
  Pallas kernels: 0 us -> 141 us
  matrix products: 56.5 us -> 0 us
  between operations: 16.3 us -> 0.01 us
  other arithmetic: 12.1 us -> 0 us
  local copies, waits for them, and re-layouts: 15.5 us -> 3.76 us
    all_gather x5 -> x0, waiting for transfers between devices: 224 us -> none  [gather_iterate(): return lax.all_gather(current, ('pix', 'chan'), axis=0, tiled=True)]
    pallas_call x0 -> x1, Pallas kernels: none -> 141 us  [body(): pl.pallas_call(kernel, out_shape=jax.ShapeDtypeStruct(facets.shape, F32),...]
    reduce_scatter x1 -> x0, waiting for transfers between devices: 82.2 us -> none  [body(): lax.psum_scatter(lax.dot_general(spectra, spectra, (((0,), (0,)), ((), ()...]
    all_to_all x2 -> x0, blocking collectives: 81.3 us -> none  [the longest x1 41.3 us: body(): lax.all_to_all(weighted, 'chan', split_axis=0, concat_axis=1, tiled=True)]
    psum x1 -> x0, blocking collectives: 61.8 us -> none  [body(): lax.psum((trace_part, square_part), ('pix', 'chan'))]
    dot_general x11 -> x0, matrix products: 56.5 us -> none  [the longest x4 19.5 us: body(): jnp.dot(current, gathered, precision=highest, preferred_element_type=jnp....]
    ppermute x2 -> x0, waiting for transfers between devices: 15.2 us -> none  [the longest x1 8.22 us: extended(): lax.ppermute(lax.slice_in_dim(block, 0, width, axis=dim), axis, backward)]
    all_to_all x3 -> x0, local copies, waits for them, and re-layouts: 7.61 us -> none  [body(): lax.all_to_all(weighted, 'chan', split_axis=0, concat_axis=1, tiled=True)]
  transfers between devices with their start and end apart: 8 -> 0, of which waited for: 8 -> 0; matrix products, arithmetic and copies ran while one was open for 2% -> 0% of each run, Pallas kernels for 0% -> 0%
where the time goes in v1:
time: 147 us; the launch traced here: 145 us
  Pallas kernels  141 us (96%)
  local copies, waits for them, and re-layouts  3.76 us (3%)
    pallas_call x1, Pallas kernels, body(): pl.pallas_call(kernel, out_shape=jax.ShapeDtypeStruct(facets.shape, F32),...  141 us
    unnamed x1, local copies, waits for them, and re-layouts  3.76 us

profile of v1, /device:TPU:1, one launch (start us, length us, event | category | flops | bytes accessed | tf_op | source)
XLA Modules:
  0.0 144.6 jit_solution(12148354562013583572)
XLA Ops:
  0.0 140.9 %facet_filter.1 = f32[1,3,1024,256]{3,2,1,0:T(8,128)} custom-call(f32[1,3,1024,256]{3,2,1,0:T(8,128)} %facets.1, f32[8,1024]{1,0:T(8,128)} %profiles.1, s32[1,3]{1,0:T(1,128)} %index.1), custom_call_target="tpu_custom_call" | custom-call | flops 60000002048 | bytes 6291456 | tf_op jit(solution)/shard_map/facet_filter/pallas_call | solution.py:478
  140.9 3.8 %copy.5 = f32[1,3,1024,256]{3,2,1,0:T(8,128)} copy(f32[1,3,1024,256]{3,2,1,0:T(8,128)} %facet_filter.1) | data formatting | bytes 6291456

commit v2 on v1

--- a/solution.py
+++ b/solution.py
@@ -21,6 +21,7 @@
 BLOCKS = 4
 CHANNELS = BLOCK * BLOCKS
 PIXELS = ROWS * BLOCK
+STRIPS = 4
 PAIRS = [(0, 0), (1, 1), (2, 2), (3, 3), (0, 1), (1, 2), (2, 3), (3, 0), (0, 2), (1, 3)]
 TILES = len(PAIRS)
 
@@ -46,11 +47,11 @@
 def kernel(
     facets, profiles, index, out,
     cube, weight, pix_hl, pix_t_hl, gram, total, from_core, from_z1, from_z2, from_x,
-    signs, square, proj, result, border,
+    signs, square, latest, proj, result, border, outgoing, incoming,
     send_near, recv_near, send_far, recv_far, own_sem,
     send_core, recv_core, send_z, recv_z, send_x, recv_x,
     send_xg, recv_xg, send_zg, recv_zg, send_cg, recv_cg,
-    send_border, recv_border, out_sem,
+    send_border, recv_border, out_sem, send_tiles, recv_tiles,
 ):
     f = lax.axis_index("facet")
     p = lax.axis_index("pix")
@@ -115,25 +116,28 @@
         there = cube.at[across, :, piece(q, way), :]
         remote(there, there, send_far.at[way, q], recv_far.at[way, q], at_x(toward[way])).wait_recv()
 
+    def place(way, q):
+        return (4 - q) % 4 if way == 0 else (q + 1) % 4
+
     def quarter(way, step):
-        if way == 0:
-            place = (4 - right) % 4
-            n = step + jnp.where(place <= step, 1, 0)
-            return (4 - n) % 4
-        place = (left + 1) % 4
-        n = step + jnp.where(place <= step, 1, 0)
-        return (3 + n) % 4
-
-    def near_round(step):
+        n = step + jnp.where(place(way, toward[way]) <= step, 1, 0)
+        return (4 - n) % 4 if way == 0 else (3 + n) % 4
+
+    def near_item(item, strips=(0, STRIPS)):
         for way in (0, 1):
-            q = quarter(way, step)
-            for h in (way, 1 - way):
-                if h == way:
-                    @pl.when(q != across)
-                    def _():
-                        near(way, q, h).start()
-                else:
-                    near(way, q, h).start()
+            n = place(way, across)
+            skipped = 2 * (n - jnp.where(place(way, toward[way]) <= n, 1, 0))
+            m = item + jnp.where(skipped <= item, 1, 0)
+            h = m % 2 if way == 0 else 1 - m % 2
+            q = quarter(way, m // 2)
+            width = HALF // STRIPS
+            strip = pl.ds(
+                pl.multiple_of(q * BLOCK + h * HALF + strips[0] * width, width), (strips[1] - strips[0]) * width
+            )
+            remote(
+                facets.at[0, :, strip, :], cube.at[a, :, strip, :],
+                send_near.at[way, q, h], recv_near.at[way, q, h], at_x(toward[way]),
+            ).start()
 
     def far_round(step):
         for way in (0, 1):
@@ -145,12 +149,11 @@
 
             far(way, q).start()
 
-    for way in (0, 1):
-        near(way, toward[way], way).start()
+    for h in (0, 1):
+        for way in (0, 1):
+            near(way, toward[way], h).start()
     for way in (0, 1):
         near(way, across, way).start()
-    for way in (0, 1):
-        near(way, toward[way], 1 - way).start()
     own = pltpu.make_async_copy(facets.at[0], cube.at[a], own_sem)
     own.start()
 
@@ -164,72 +167,106 @@
 
     mine = pl.ds(pl.multiple_of(a * BLOCK, BLOCK), BLOCK)
 
-    def spectra(b):
-        columns = pl.ds(pl.multiple_of(b * BLOCK, BLOCK), BLOCK)
+    def spectra(b, distance):
         for r in range(ROWS):
             w = weight[r, mine, :]
             x = cube[b, r, mine, :] * jnp.concatenate([w, w], axis=1)
             high, low = split(x)
-            pix_hl[0, block(r), columns] = high
-            pix_hl[1, block(r), columns] = low
+            pix_hl[0, block(r), block(distance)] = high
+            pix_hl[1, block(r), block(distance)] = low
             high, low = split(x.T)
-            pix_t_hl[0, columns, block(r)] = high
-            pix_t_hl[1, columns, block(r)] = low
-
-    spectra(a)
+            pix_t_hl[0, block(distance), block(r)] = high
+            pix_t_hl[1, block(distance), block(r)] = low
+
+    def gram_tile(slot, i, j):
+        gram[slot] = dot3(pix_t_hl[0, i, :], pix_t_hl[1, i, :], pix_hl[0, :, j], pix_hl[1, :, j])
+
+    def distant(d):
+        return pl.ds(pl.multiple_of(d * BLOCK, BLOCK), BLOCK)
+
+    SPANS = [pl.ds(0, 6), pl.ds(6, 4)]
+
+    def rows(start, count):
+        return pl.ds(pl.multiple_of(start, 8), count)
+
+    half = k * 128
+
+    def part(zz):
+        return half + zz * 32
+
+    def swap(e):
+        return remote(
+            gram.at[SPANS[e], rows((1 - k) * 128, 128), :], from_core.at[SPANS[e]],
+            send_core.at[e], recv_core.at[e], core_mate,
+        )
+
+    def sixteen(e, zz, h):
+        return gram.at[SPANS[e], rows(part(zz) + 16 * h, 16), :]
+
+    z_to = [z_up, z_down]
+
+    def first(e, way):
+        return remote(
+            sixteen(e, z_across, way), from_z1.at[way, SPANS[e]],
+            send_z.at[e, way, 0], recv_z.at[e, way, 0], at_z(z_to[way]),
+        )
+
+    def second(e, way, h):
+        return remote(
+            sixteen(e, z_to[way], h), from_z2.at[way, h, SPANS[e]],
+            send_z.at[e, way, 1 + h], recv_z.at[e, way, 1 + h], at_z(z_to[way]),
+        )
+
+    def cores_summed(e):
+        swap(e).start()
+        swap(e).wait()
+        gram[SPANS[e], rows(half, 128), :] += from_core[SPANS[e]]
+        for way in (0, 1):
+            first(e, way).start()
+        for way in (0, 1):
+            second(e, way, 1 - way).start()
+
+    def z_summed(e):
+        for way in (0, 1):
+            first(e, way).wait_recv()
+            gram[SPANS[e], rows(part(z_to[way]) + 16 * way, 16), :] += from_z1[way, SPANS[e]]
+            second(e, way, way).start()
+        for h in (0, 1):
+            second(e, 0, h).wait_recv()
+            second(e, 1, h).wait_recv()
+            gram[SPANS[e], rows(part(z) + 16 * h, 16), :] += from_z2[0, h, SPANS[e]] + from_z2[1, h, SPANS[e]]
+
+    spectra(a, 0)
+    gram_tile(1, block(0), block(0))
+    for way in (0, 1):
+        wait_near(way, a, 0)
+        wait_near(way, a, 1)
+    spectra(left, 3)
+    spectra(right, 1)
+    gram_tile(0, block(3), block(3))
+    gram_tile(2, block(1), block(1))
+    gram_tile(3, block(3), block(0))
+    gram_tile(4, block(0), block(1))
+    side = jnp.where((a == 0) | (a == 3), 1, 3)
+    gram_tile(5, distant(side), distant(4 - side))
+    cores_summed(0)
     for way in (0, 1):
         wait_near(way, toward[way], way)
         far(way, toward[way]).start()
-    for way in (0, 1):
-        wait_near(way, a, 0)
-        wait_near(way, a, 1)
-    spectra(left)
-    spectra(right)
+    near_item(0)
+    z_summed(0)
     for way in (0, 1):
         wait_far(way, a)
-    near_round(0)
-    spectra(across)
-
-    for t, (i, j) in enumerate(PAIRS):
-        gram[t] = dot3(
-            pix_t_hl[0, block(i), :], pix_t_hl[1, block(i), :], pix_hl[0, :, block(j)], pix_hl[1, :, block(j)]
-        )
-
-    def rows(start, count):
-        return pl.ds(pl.multiple_of(start, 8), count)
-
-    half = k * 128
-    swap = remote(
-        gram.at[:, rows((1 - k) * 128, 128), :], from_core, send_core, recv_core, core_mate
-    )
-    swap.start()
-    swap.wait()
-
-    def part(zz):
-        return half + zz * 32
-
-    gram[:, rows(half, 128), :] += from_core[...]
-
-    first = [
-        remote(gram.at[:, rows(part(z_across), 16), :], from_z1.at[0], send_z.at[0], recv_z.at[0], at_z(z_up)),
-        remote(gram.at[:, rows(part(z_across) + 16, 16), :], from_z1.at[1], send_z.at[1], recv_z.at[1], at_z(z_down)),
-    ]
-    for copy in first:
-        copy.start()
-    for copy in first:
-        copy.wait()
-    gram[:, rows(part(z_up), 16), :] += from_z1[0]
-    gram[:, rows(part(z_down) + 16, 16), :] += from_z1[1]
-    second = [
-        remote(gram.at[:, rows(part(z_up), 32), :], from_z2.at[0], send_z.at[2], recv_z.at[2], at_z(z_up)),
-        remote(gram.at[:, rows(part(z_down), 32), :], from_z2.at[1], send_z.at[3], recv_z.at[3], at_z(z_down)),
-    ]
-    for copy in second:
-        copy.start()
-    for copy in second:
-        copy.wait()
+    spectra(across, 2)
+    gram_tile(6, block(2), block(2))
+    gram_tile(7, block(1), block(2))
+    gram_tile(8, block(2), block(3))
+    side = jnp.where(a < 2, 0, 2)
+    gram_tile(9, distant(side), distant(2 - side))
+    cores_summed(1)
+    near_item(1, (0, 2))
+    z_summed(1)
     base = part(z)
-    gram[:, rows(base, 32), :] += from_z2[0] + from_z2[1]
 
     scatter = []
     for d in (1, 2, 3):
@@ -240,10 +277,28 @@
         ))
     for copy in scatter:
         copy.start()
+    near_item(1, (2, 3))
     for copy in scatter:
         copy.wait()
     own_rows = rows(base + a * 8, 8)
-    total[:, own_rows, :] = (gram[:, own_rows, :] + from_x[0]) + (from_x[1] + from_x[2])
+
+    def pick(n, values):
+        result = values[0]
+        for m in range(1, len(values)):
+            result = jnp.where(n == m, values[m], result)
+        return result
+
+    def slot(chan, t):
+        if t < 4:
+            return pick((t + 4 - chan) % 4, [1, 2, 6, 0])
+        if t < 8:
+            return pick((t - chan) % 4, [4, 7, 8, 3])
+        return pick((t + chan) % 2, [9, 5])
+
+    for t in range(TILES):
+        total[t, own_rows, :] = (
+            gram[slot(a, t), own_rows, :] + from_x[0, slot(left, t)]
+        ) + (from_x[1, slot(across, t)] + from_x[2, slot(right, t)])
 
     def gather_x(d):
         return remote(
@@ -272,20 +327,26 @@
     def to_mate(ref, slot):
         return remote(ref, ref, send_cg.at[slot], recv_cg.at[slot], core_mate)
 
-    along(whole(z), 0, at_z(z_up)).start()
-    along(whole(z), 1, at_z(z_down)).start()
+    along(low_half(z), 0, at_z(z_up)).start()
+    along(high_half(z), 3, at_z(z_down)).start()
+    along(high_half(z), 1, at_z(z_up)).start()
+    along(low_half(z), 4, at_z(z_down)).start()
     to_mate(whole(z), 0).start()
+    near_item(1, (3, 4))
     far_round(0)
-    near_round(1)
-    near_round(2)
-    along(whole(z_down), 0, at_z(z_up)).wait_recv()
+    near_item(2)
+    near_item(3)
+    near_item(4)
+    along(low_half(z_down), 0, at_z(z_up)).wait_recv()
     along(low_half(z_down), 2, at_z(z_up)).start()
+    along(high_half(z_up), 3, at_z(z_down)).wait_recv()
+    along(high_half(z_up), 5, at_z(z_down)).start()
+    along(high_half(z_down), 1, at_z(z_up)).wait_recv()
     to_mate(whole(z_down), 1).start()
-    along(whole(z_up), 1, at_z(z_down)).wait_recv()
-    along(high_half(z_up), 3, at_z(z_down)).start()
+    along(low_half(z_up), 4, at_z(z_down)).wait_recv()
     to_mate(whole(z_up), 2).start()
     along(low_half(z_across), 2, at_z(z_up)).wait_recv()
-    along(high_half(z_across), 3, at_z(z_down)).wait_recv()
+    along(high_half(z_across), 5, at_z(z_down)).wait_recv()
     to_mate(whole(z_across), 3).start()
 
     def mate_whole(zz):
@@ -315,66 +376,87 @@
         squares = term if squares is None else squares + term
     spread = jnp.sqrt(add_up(squares) + EPSILON)
 
-    def put(ref, lead, i, j, tile):
+    def put(ref, lead, i, j, tile, mirror):
         high, low = split(tile)
-        ref[lead + (0, block(i), block(j))] = high
-        ref[lead + (1, block(i), block(j))] = low
-        if i != j:
+        ref[lead + (0, i, j)] = high
+        ref[lead + (1, i, j)] = low
+        if mirror:
             high, low = split(tile.T)
-            ref[lead + (0, block(j), block(i))] = high
-            ref[lead + (1, block(j), block(i))] = low
+            ref[lead + (0, j, i)] = high
+            ref[lead + (1, j, i)] = low
+
+    def local(b):
+        return pl.ds(pl.multiple_of(((b + 2 * k) % 4) * BLOCK, BLOCK), BLOCK)
 
     for t, (i, j) in enumerate(PAIRS):
         tile = total[t]
         if i == j:
             tile = tile - mean_eig * eye
-        tile = tile / spread
-        gram[t] = tile
-        put(signs, (0,), i, j, tile)
-
-    def iterate(step, _):
+        put(signs, (0,), local(i), local(j), tile / spread, i != j)
+
+    own_tiles = [(0, 0), (0, 1), (1, 1)]
+    cross_tiles = [(0, 2), (0, 3), (1, 2), (1, 3)]
+
+    def trade(step):
+        return remote(outgoing.at[step], incoming.at[step], send_tiles.at[step], recv_tiles.at[step], core_mate)
+
+    def absorb(step, buffer):
+        trade(step).wait_recv()
+        for n, (i, j) in enumerate(own_tiles):
+            put(signs, (buffer,), block(i + 2), block(j + 2), incoming[step, n], i != j)
+
+    for step in range(ITERS - 1):
         now = step % 2
         later = 1 - now
 
-        @pl.when(step == 1)
-        def _():
-            far_round(1)
-
-        @pl.when(step == 2)
-        def _():
-            far_round(2)
-
-        for i, j in PAIRS:
-            put(square, (), i, j, dot3(
+        def squared(i, j):
+            return dot3(
                 signs[now, 0, block(i), :], signs[now, 1, block(i), :],
                 signs[now, 0, :, block(j)], signs[now, 1, :, block(j)],
-            ))
-        for t, (i, j) in enumerate(PAIRS):
+            )
+
+        def renewed(i, j):
             cubic = dot3(
-                signs[now, 0, block(i), :], signs[now, 1, block(i), :],
-                square[0, :, block(j)], square[1, :, block(j)],
+                square[0, block(i), :], square[1, block(i), :],
+                signs[now, 0, :, block(j)], signs[now, 1, :, block(j)],
             )
-            tile = 1.5 * gram[t] - 0.5 * cubic
-            gram[t] = tile
-            put(signs, (later,), i, j, tile)
-        return 0
-
-    lax.fori_loop(0, ITERS - 1, iterate, 0)
+            current = signs[now, 0, block(i), block(j)].astype(F32) + signs[now, 1, block(i), block(j)].astype(F32)
+            return 1.5 * current - 0.5 * cubic
+
+        for i, j in own_tiles:
+            put(square, (), block(i), block(j), squared(i, j), i != j)
+
+        if step > 0:
+            absorb(step - 1, now)
+        if step == 2:
+            far_round(1)
+
+        for i, j in cross_tiles:
+            put(square, (), block(i), block(j), squared(i, j), False)
+        for n, (i, j) in enumerate(own_tiles):
+            tile = renewed(i, j)
+            outgoing[step, n] = tile
+            put(signs, (later,), block(i), block(j), tile, i != j)
+        trade(step).start()
+        for i, j in cross_tiles:
+            put(signs, (later,), block(i), block(j), renewed(i, j), True)
 
     last = (ITERS - 1) % 2
+    absorb(ITERS - 2, last)
+    far_round(2)
+    here = local(a)
     for i in range(BLOCKS):
         high, low = split(dot3(
             signs[last, 0, block(i), :], signs[last, 1, block(i), :],
-            signs[last, 0, :, mine], signs[last, 1, :, mine],
+            signs[last, 0, :, here], signs[last, 1, :, here],
         ))
-        square[0, block(i), 0:BLOCK] = high
-        square[1, block(i), 0:BLOCK] = low
+        latest[0, block(i), :] = high
+        latest[1, block(i), :] = low
     for i in range(BLOCKS):
         cubic = dot3(
-            signs[last, 0, block(i), :], signs[last, 1, block(i), :],
-            square[0, :, 0:BLOCK], square[1, :, 0:BLOCK],
-        )
-        current = signs[last, 0, block(i), mine].astype(F32) + signs[last, 1, block(i), mine].astype(F32)
+            signs[last, 0, block(i), :], signs[last, 1, block(i), :], latest[0], latest[1],
+        )
+        current = signs[last, 0, block(i), here].astype(F32) + signs[last, 1, block(i), here].astype(F32)
         high, low = split(1.5 * current - 0.5 * cubic)
         proj[0, block(i), :] = high
         proj[1, block(i), :] = low
@@ -387,7 +469,7 @@
                 wait_far(way, q)
 
         for r in range(ROWS):
-            x = jnp.concatenate([cube[b, r, block(q), :] for b in range(BLOCKS)], axis=1)
+            x = jnp.concatenate([cube[(b + 2 * k) % 4, r, block(q), :] for b in range(BLOCKS)], axis=1)
             high, low = split(x)
             product = dot3(high, low, proj[0], proj[1])
             w = weight[r, block(q), :]
@@ -442,10 +524,19 @@
             far(way, q).wait_send()
     for d in (1, 2, 3):
         gather_x(d).wait_send()
-    along(whole(z), 0, at_z(z_up)).wait_send()
-    along(whole(z), 1, at_z(z_down)).wait_send()
+    for way in (0, 1):
+        for e in (0, 1):
+            first(e, way).wait_send()
+            for h in (0, 1):
+                second(e, way, h).wait_send()
+    along(low_half(z), 0, at_z(z_up)).wait_send()
+    along(high_half(z), 1, at_z(z_up)).wait_send()
     along(low_half(z_down), 2, at_z(z_up)).wait_send()
-    along(high_half(z_up), 3, at_z(z_down)).wait_send()
+    along(high_half(z), 3, at_z(z_down)).wait_send()
+    along(low_half(z), 4, at_z(z_down)).wait_send()
+    along(high_half(z_up), 5, at_z(z_down)).wait_send()
+    for step in range(ITERS - 1):
+        trade(step).wait_send()
     for slot, zz in enumerate((z, z_down, z_up, z_across)):
         to_mate(whole(zz), slot).wait_send()
     for q in range(BLOCKS):
@@ -463,17 +554,20 @@
         pltpu.VMEM((TILES, BLOCK, BLOCK), F32),
         pltpu.VMEM((TILES, 128, BLOCK), F32),
         pltpu.VMEM((2, TILES, 16, BLOCK), F32),
-        pltpu.VMEM((2, TILES, 32, BLOCK), F32),
+        pltpu.VMEM((2, 2, TILES, 16, BLOCK), F32),
         pltpu.VMEM((3, TILES, 8, BLOCK), F32),
         pltpu.VMEM((2, 2, CHANNELS, CHANNELS), BF16),
-        pltpu.VMEM((2, CHANNELS, CHANNELS), BF16),
+        pltpu.VMEM((2, 2 * BLOCK, CHANNELS), BF16),
+        pltpu.VMEM((2, CHANNELS, BLOCK), BF16),
         pltpu.VMEM((2, CHANNELS, BLOCK), BF16),
         pltpu.VMEM((ROWS, COLS, BLOCK), F32),
         pltpu.VMEM((2, ROWS, OV, BLOCK), F32),
+        pltpu.VMEM((ITERS - 1, 3, BLOCK, BLOCK), F32),
+        pltpu.VMEM((ITERS - 1, 3, BLOCK, BLOCK), F32),
         dma((2, 4, 2)), dma((2, 4, 2)), dma((2, 4)), dma((2, 4)), dma,
-        dma, dma, dma((4,)), dma((4,)), dma((3,)), dma((3,)),
-        dma((3,)), dma((3,)), dma((4,)), dma((4,)), dma((4,)), dma((4,)),
-        dma((2,)), dma((2,)), dma((4,)),
+        dma((2,)), dma((2,)), dma((2, 2, 3)), dma((2, 2, 3)), dma((3,)), dma((3,)),
+        dma((3,)), dma((3,)), dma((6,)), dma((6,)), dma((4,)), dma((4,)),
+        dma((2,)), dma((2,)), dma((4,)), dma((ITERS - 1,)), dma((ITERS - 1,)),
     ]
     return pl.pallas_call(
         kernel,

time: 147 us -> 131 us (0.89)
  Pallas kernels: 141 us -> 126 us
    pallas_call x1, Pallas kernels: 141 us -> 126 us  [body(): pl.pallas_call(kernel, out_shape=jax.ShapeDtypeStruct(facets.shape, F32),...]
where the time goes in v2:
time: 131 us; the launch traced here: 130 us
  Pallas kernels  126 us (96%)
  local copies, waits for them, and re-layouts  3.76 us (3%)
    pallas_call x1, Pallas kernels, body(): pl.pallas_call(kernel, out_shape=jax.ShapeDtypeStruct(facets.shape, F32),...  126 us
    unnamed x1, local copies, waits for them, and re-layouts  3.76 us

profile of v2, /device:TPU:1, one launch (start us, length us, event | category | flops | bytes accessed | tf_op | source)
XLA Modules:
  0.0 129.9 jit_solution(10563147923330252426)
XLA Ops:
  0.0 126.1 %facet_filter.1 = f32[1,3,1024,256]{3,2,1,0:T(8,128)} custom-call(f32[1,3,1024,256]{3,2,1,0:T(8,128)} %facets.1, f32[8,1024]{1,0:T(8,128)} %profiles.1, s32[1,3]{1,0:T(1,128)} %index.1), custom_call_target="tpu_custom_call" | custom-call | flops 60000002048 | bytes 6291456 | tf_op jit(solution)/shard_map/facet_filter/pallas_call | solution.py:572
  126.1 3.8 %copy.5 = f32[1,3,1024,256]{3,2,1,0:T(8,128)} copy(f32[1,3,1024,256]{3,2,1,0:T(8,128)} %facet_filter.1) | data formatting | bytes 6291456

commit v3 on v2

--- a/solution.py
+++ b/solution.py
@@ -308,6 +308,10 @@
 
     for d in (1, 2, 3):
         gather_x(d).start()
+    near_item(1, (3, 4))
+    far_round(0)
+    near_item(2)
+    near_item(3)
     for d in (1, 2, 3):
         there = total.at[:, rows(base + ((a + 4 - d) % 4) * 8, 8), :]
         remote(there, there, send_xg.at[d - 1], recv_xg.at[d - 1], at_x((a + d) % 4)).wait_recv()
@@ -332,11 +336,6 @@
     along(high_half(z), 1, at_z(z_up)).start()
     along(low_half(z), 4, at_z(z_down)).start()
     to_mate(whole(z), 0).start()
-    near_item(1, (3, 4))
-    far_round(0)
-    near_item(2)
-    near_item(3)
-    near_item(4)
     along(low_half(z_down), 0, at_z(z_up)).wait_recv()
     along(low_half(z_down), 2, at_z(z_up)).start()
     along(high_half(z_up), 3, at_z(z_down)).wait_recv()
@@ -428,8 +427,9 @@
 
         if step > 0:
             absorb(step - 1, now)
-        if step == 2:
+        if step == 1:
             far_round(1)
+            near_item(4)
 
         for i, j in cross_tiles:
             put(square, (), block(i), block(j), squared(i, j), False)
@@ -458,64 +458,109 @@
         )
         current = signs[last, 0, block(i), here].astype(F32) + signs[last, 1, block(i), here].astype(F32)
         high, low = split(1.5 * current - 0.5 * cubic)
-        proj[0, block(i), :] = high
-        proj[1, block(i), :] = low
-
-    def filtered(q):
+        distance = ((i + 2 * k) % 4 + 4 - a) % 4
+        row = pl.ds(pl.multiple_of(jnp.where(distance < 2, distance, 5 - distance) * BLOCK, BLOCK), BLOCK)
+        proj[0, row, :] = high
+        proj[1, row, :] = low
+
+    def at_hand(q, last_too):
         @pl.when(q != a)
         def _():
             for way in (0, 1):
                 wait_near(way, q, 1 - way)
+                if last_too:
+                    wait_far(way, q)
+
+    def scale(r, columns):
+        w = weight[r, columns, :]
+        w = 0.5 * (w * w)
+        return jnp.concatenate([w, w], axis=1)
+
+    blocks = [a, right, left, across]
+    inner = BLOCK * 3
+
+    def filtered_pair(r, low, high):
+        x = jnp.concatenate(
+            [jnp.concatenate([cube[b, r, low, :], cube[b, r, high, :]], axis=0) for b in blocks], axis=1
+        )
+        x_high, x_low = split(x)
+        product = dot3(x_high, x_low, proj[0], proj[1])
+        result[r, low, :] = (cube[a, r, low, :] + product[0:HALF]) * scale(r, low)
+        result[r, high, :] = (cube[a, r, high, :] + product[HALF:]) * scale(r, high)
+
+    def begun(q):
+        for r in range(ROWS):
+            high, low = split(jnp.concatenate([cube[b, r, block(q), :] for b in blocks[:3]], axis=1))
+            product = dot3(high, low, proj[0, 0:inner, :], proj[1, 0:inner, :])
+            result[r, block(q), :] = cube[a, r, block(q), :] + product
+
+    def finished(q):
+        for r in range(ROWS):
+            high, low = split(cube[across, r, block(q), :])
+            product = dot3(high, low, proj[0, inner:, :], proj[1, inner:, :])
+            result[r, block(q), :] = (result[r, block(q), :] + product) * scale(r, block(q))
+
+    def to_hbm(n, r, start, width):
+        there = (r, pl.ds(start, width), slice(None))
+        return pltpu.make_async_copy(result.at[there], out.at[(0,) + there], out_sem.at[n])
+
+    low_rim = slice(0, OV)
+    high_rim = slice(COLS - OV, COLS)
+    down = [
+        remote(result.at[r, low_rim, :], border.at[1, r], send_border.at[0, r], recv_border.at[0, r], facet_down)
+        for r in range(ROWS)
+    ]
+    up = [
+        remote(result.at[r, high_rim, :], border.at[0, r], send_border.at[1, r], recv_border.at[1, r], facet_up)
+        for r in range(ROWS)
+    ]
+    at_hand(0, True)
+    at_hand(3, True)
+    for r in range(ROWS):
+        filtered_pair(r, low_rim, high_rim)
+
+        @pl.when(f > 0)
+        def _():
+            down[r].start()
+
+        @pl.when(f < 3)
+        def _():
+            up[r].start()
+
+    for r in range(ROWS):
+        filtered_pair(r, slice(OV, BLOCK), slice(COLS - BLOCK, COLS - OV))
+    at_hand(1, False)
+    at_hand(2, False)
+    begun(1)
+    begun(2)
+    for q in (1, 2):
+        @pl.when(q != a)
+        def _():
+            for way in (0, 1):
                 wait_far(way, q)
 
-        for r in range(ROWS):
-            x = jnp.concatenate([cube[(b + 2 * k) % 4, r, block(q), :] for b in range(BLOCKS)], axis=1)
-            high, low = split(x)
-            product = dot3(high, low, proj[0], proj[1])
-            w = weight[r, block(q), :]
-            w = 0.5 * (w * w)
-            result[r, block(q), :] = (cube[a, r, block(q), :] + product) * jnp.concatenate([w, w], axis=1)
-
-    def to_hbm(q):
-        there = (slice(None), block(q), slice(None))
-        return pltpu.make_async_copy(result.at[there], out.at[(0,) + there], out_sem.at[q])
-
-    low_rim = result.at[:, 0:OV, :]
-    high_rim = result.at[:, COLS - OV : COLS, :]
-    down = remote(low_rim, border.at[1], send_border.at[0], recv_border.at[0], facet_down)
-    up = remote(high_rim, border.at[0], send_border.at[1], recv_border.at[1], facet_up)
-
-    filtered(0)
-
-    @pl.when(f > 0)
-    def _():
-        down.start()
-
-    filtered(3)
-
-    @pl.when(f < 3)
-    def _():
-        up.start()
-
-    for q in (1, 2):
-        filtered(q)
-        to_hbm(q).start()
-
-    @pl.when(f > 0)
-    def _():
-        down.wait_send()
-        up.wait_recv()
-        result[:, 0:OV, :] += border[0]
-
-    to_hbm(0).start()
-
-    @pl.when(f < 3)
-    def _():
-        up.wait_send()
-        down.wait_recv()
-        result[:, COLS - OV : COLS, :] += border[1]
-
-    to_hbm(3).start()
+        finished(q)
+
+    writes = []
+    for r in range(ROWS):
+        writes.append(to_hbm(len(writes), r, OV, COLS - 2 * OV))
+        writes[-1].start()
+    for r in range(ROWS):
+        @pl.when(f > 0)
+        def _():
+            down[r].wait_send()
+            up[r].wait_recv()
+            result[r, low_rim, :] += border[0, r]
+
+        @pl.when(f < 3)
+        def _():
+            up[r].wait_send()
+            down[r].wait_recv()
+            result[r, high_rim, :] += border[1, r]
+
+        for start in (0, COLS - OV):
+            writes.append(to_hbm(len(writes), r, start, OV))
+            writes[-1].start()
 
     for way in (0, 1):
         for q in range(BLOCKS):
@@ -539,8 +584,8 @@
         trade(step).wait_send()
     for slot, zz in enumerate((z, z_down, z_up, z_across)):
         to_mate(whole(zz), slot).wait_send()
-    for q in range(BLOCKS):
-        to_hbm(q).wait()
+    for write in writes:
+        write.wait()
 
 
 def body(facets, profiles, profile_index):
@@ -567,7 +612,7 @@
         dma((2, 4, 2)), dma((2, 4, 2)), dma((2, 4)), dma((2, 4)), dma,
         dma((2,)), dma((2,)), dma((2, 2, 3)), dma((2, 2, 3)), dma((3,)), dma((3,)),
         dma((3,)), dma((3,)), dma((6,)), dma((6,)), dma((4,)), dma((4,)),
-        dma((2,)), dma((2,)), dma((4,)), dma((ITERS - 1,)), dma((ITERS - 1,)),
+        dma((2, ROWS)), dma((2, ROWS)), dma((3 * ROWS,)), dma((ITERS - 1,)), dma((ITERS - 1,)),
     ]
     return pl.pallas_call(
         kernel,

time: 131 us -> 128 us (0.977)
  Pallas kernels: 126 us -> 124 us
    pallas_call x1, Pallas kernels: 126 us -> 124 us  [body(): pl.pallas_call(kernel, out_shape=jax.ShapeDtypeStruct(facets.shape, F32),...]
where the time goes in v3:
time: 128 us
  Pallas kernels  124 us (97%)
  local copies, waits for them, and re-layouts  3.76 us (3%)
    pallas_call x1, Pallas kernels, body(): pl.pallas_call(kernel, out_shape=jax.ShapeDtypeStruct(facets.shape, F32),...  124 us
    unnamed x1, local copies, waits for them, and re-layouts  3.76 us

profile of v3, /device:TPU:1, one launch (start us, length us, event | category | flops | bytes accessed | tf_op | source)
XLA Modules:
  0.0 128.0 jit_solution(10750962402934402472)
XLA Ops:
  0.0 124.2 %facet_filter.1 = f32[1,3,1024,256]{3,2,1,0:T(8,128)} custom-call(f32[1,3,1024,256]{3,2,1,0:T(8,128)} %facets.1, f32[8,1024]{1,0:T(8,128)} %profiles.1, s32[1,3]{1,0:T(1,128)} %index.1), custom_call_target="tpu_custom_call" | custom-call | flops 60000002048 | bytes 6291456 | tf_op jit(solution)/shard_map/facet_filter/pallas_call | solution.py:617
  124.2 3.8 %copy.5 = f32[1,3,1024,256]{3,2,1,0:T(8,128)} copy(f32[1,3,1024,256]{3,2,1,0:T(8,128)} %facet_filter.1) | data formatting | bytes 6291456

commit v4 on v3

--- a/solution.py
+++ b/solution.py
@@ -226,11 +226,13 @@
         for way in (0, 1):
             second(e, way, 1 - way).start()
 
-    def z_summed(e):
+    def z_forwarded(e):
         for way in (0, 1):
             first(e, way).wait_recv()
             gram[SPANS[e], rows(part(z_to[way]) + 16 * way, 16), :] += from_z1[way, SPANS[e]]
             second(e, way, way).start()
+
+    def z_summed(e):
         for h in (0, 1):
             second(e, 0, h).wait_recv()
             second(e, 1, h).wait_recv()
@@ -254,7 +256,7 @@
         wait_near(way, toward[way], way)
         far(way, toward[way]).start()
     near_item(0)
-    z_summed(0)
+    z_forwarded(0)
     for way in (0, 1):
         wait_far(way, a)
     spectra(across, 2)
@@ -265,6 +267,8 @@
     gram_tile(9, distant(side), distant(2 - side))
     cores_summed(1)
     near_item(1, (0, 2))
+    z_summed(0)
+    z_forwarded(1)
     z_summed(1)
     base = part(z)
 
@@ -430,6 +434,8 @@
         if step == 1:
             far_round(1)
             near_item(4)
+        if step == 2:
+            far_round(2)
 
         for i, j in cross_tiles:
             put(square, (), block(i), block(j), squared(i, j), False)
@@ -443,7 +449,6 @@
 
     last = (ITERS - 1) % 2
     absorb(ITERS - 2, last)
-    far_round(2)
     here = local(a)
     for i in range(BLOCKS):
         high, low = split(dot3(
@@ -514,6 +519,12 @@
         remote(result.at[r, high_rim, :], border.at[0, r], send_border.at[1, r], recv_border.at[1, r], facet_up)
         for r in range(ROWS)
     ]
+    writes = []
+
+    def write_out(r, start, width):
+        writes.append(to_hbm(len(writes), r, start, width))
+        writes[-1].start()
+
     at_hand(0, True)
     at_hand(3, True)
     for r in range(ROWS):
@@ -529,6 +540,8 @@
 
     for r in range(ROWS):
         filtered_pair(r, slice(OV, BLOCK), slice(COLS - BLOCK, COLS - OV))
+        for start in (OV, COLS - BLOCK):
+            write_out(r, start, HALF)
     at_hand(1, False)
     at_hand(2, False)
     begun(1)
@@ -540,11 +553,9 @@
                 wait_far(way, q)
 
         finished(q)
-
-    writes = []
-    for r in range(ROWS):
-        writes.append(to_hbm(len(writes), r, OV, COLS - 2 * OV))
-        writes[-1].start()
+        for r in range(ROWS):
+            write_out(r, q * BLOCK, BLOCK)
+
     for r in range(ROWS):
         @pl.when(f > 0)
         def _():
@@ -559,8 +570,7 @@
             result[r, high_rim, :] += border[1, r]
 
         for start in (0, COLS - OV):
-            writes.append(to_hbm(len(writes), r, start, OV))
-            writes[-1].start()
+            write_out(r, start, OV)
 
     for way in (0, 1):
         for q in range(BLOCKS):
@@ -612,7 +622,7 @@
         dma((2, 4, 2)), dma((2, 4, 2)), dma((2, 4)), dma((2, 4)), dma,
         dma((2,)), dma((2,)), dma((2, 2, 3)), dma((2, 2, 3)), dma((3,)), dma((3,)),
         dma((3,)), dma((3,)), dma((6,)), dma((6,)), dma((4,)), dma((4,)),
-        dma((2, ROWS)), dma((2, ROWS)), dma((3 * ROWS,)), dma((ITERS - 1,)), dma((ITERS - 1,)),
+        dma((2, ROWS)), dma((2, ROWS)), dma((6 * ROWS,)), dma((ITERS - 1,)), dma((ITERS - 1,)),
     ]
     return pl.pallas_call(
         kernel,

time: 128 us -> 128 us (level)
  no operation moved by 1% of the time
where the time goes in v4:
time: 128 us
  Pallas kernels  124 us (97%)
  local copies, waits for them, and re-layouts  3.76 us (3%)
    pallas_call x1, Pallas kernels, body(): pl.pallas_call(kernel, out_shape=jax.ShapeDtypeStruct(facets.shape, F32),...  124 us
    unnamed x1, local copies, waits for them, and re-layouts  3.76 us

profile of v4, /device:TPU:1, one launch (start us, length us, event | category | flops | bytes accessed | tf_op | source)
XLA Modules:
  0.0 127.6 jit_solution(17655177172248505853)
XLA Ops:
  0.0 123.8 %facet_filter.1 = f32[1,3,1024,256]{3,2,1,0:T(8,128)} custom-call(f32[1,3,1024,256]{3,2,1,0:T(8,128)} %facets.1, f32[8,1024]{1,0:T(8,128)} %profiles.1, s32[1,3]{1,0:T(1,128)} %index.1), custom_call_target="tpu_custom_call" | custom-call | flops 60000002048 | bytes 6291456 | tf_op jit(solution)/shard_map/facet_filter/pallas_call | solution.py:627
  123.8 3.8 %copy.5 = f32[1,3,1024,256]{3,2,1,0:T(8,128)} copy(f32[1,3,1024,256]{3,2,1,0:T(8,128)} %facet_filter.1) | data formatting | bytes 6291456
